TPU v7x, 256 devices: a whole 4x4x8 slice. The times are simulated.
256 devices in a mesh: rep: 16 (over z_lo, x, core), ctx: 16 (over z_hi, y).
Axes of the slice: x: 4, y: 4, z: 8 (z_hi: 4, z_lo: 2; z = z_hi * 2 + z_lo), core: 2. Of those that a mesh axis runs over, the one named last changes fastest.
Arguments:
- query_feat: bfloat16 [16, 6144, 512], P('rep', 'ctx'), may hold values from -6 to 6
- key_feat: bfloat16 [16, 6144, 512], P('rep', 'ctx'), may hold values from -6 to 6
- value_feat: bfloat16 [16, 6144, 512], P('rep', 'ctx'), may hold values from -6 to 6
- filter_taps: float32 [6144, 512], P(None, 'ctx'), may hold values from -1.2 to 1.2
- out_cotangent: bfloat16 [16, 6144, 512], P('rep', 'ctx'), may hold values from -6 to 6
Outputs:
- operator_out: bfloat16 [16, 6144, 512], P('rep', 'ctx')
- grad_query: bfloat16 [16, 6144, 512], P('rep', 'ctx')
- grad_key: bfloat16 [16, 6144, 512], P('rep', 'ctx')
- grad_value: bfloat16 [16, 6144, 512], P('rep', 'ctx')
- grad_filter: float32 [6144, 512], P('rep', 'ctx')
All inputs are finite; a program needn't handle non-finite values.
Results may differ from a plain program's by a relative error of at most 0.022.
Values may be sent and summed in bfloat16 or wider, within the bound.
A program may use at most 64 MiB of HBM per device.

v0:
```python
import functools
import math

import jax
import jax.numpy as jnp
import ml_dtypes
import numpy as np
from jax import lax
from jax.experimental import pallas as pl
from jax.experimental.pallas import tpu as pltpu
from jax.sharding import PartitionSpec as P

MESH = pl.DeviceIdType.MESH
F32 = jnp.float32
BF16 = jnp.bfloat16
LANES = 128
HALF = 56
GROUP = 4


def split_table(table):
    high = table.astype(ml_dtypes.bfloat16)
    low = (table - high.astype(np.float64)).astype(ml_dtypes.bfloat16)
    return high, low


def wave_tables(sources):
    pieces = 3
    rows = sources * pieces
    waves = 2 * rows
    points = waves * LANES
    order = np.array([source * pieces + piece for piece in range(pieces) for source in range(sources)])
    wave = np.arange(rows + 1)
    lane = np.arange(LANES)

    first = np.zeros((2 * HALF, rows))
    angle = 2.0 * np.pi * (wave[:, None] * order[None, :] % waves) / waves
    first[: rows + 1] = np.cos(angle)
    first[HALF : HALF + rows + 1] = -np.sin(angle)

    weight = np.where((wave == 0) | (wave == rows), 1.0, 2.0) / points
    last = np.zeros((rows, 2 * HALF))
    last[:, : rows + 1] = np.cos(angle).T * weight
    last[:, HALF : HALF + rows + 1] = -np.sin(angle).T * weight

    twist = np.zeros((2, HALF, LANES))
    turn = 2.0 * np.pi * (wave[:, None] * lane[None, :] % points) / points
    twist[0, : rows + 1] = np.cos(turn)
    twist[1, : rows + 1] = np.sin(turn)

    spin = 2.0 * np.pi * (lane[:, None] * lane[None, :] % LANES) / LANES
    cos, sin = np.cos(spin), np.sin(spin)
    middle = np.block([[cos, -sin], [sin, cos]])
    back = np.block([[cos, sin], [-sin, cos]])

    first_high, first_low = split_table(first)
    last_high, last_low = split_table(last)
    return (
        np.concatenate([first_high, first_low], axis=1),
        np.concatenate([first_high, first_low, first_high], axis=1),
        np.concatenate([last_high, last_low], axis=1),
        middle.astype(ml_dtypes.bfloat16),
        back.astype(ml_dtypes.bfloat16),
        twist.astype(np.float32),
    )


def dot(left, right):
    return jnp.dot(left, right, preferred_element_type=F32)


def take_rows(wide, group, sources, channels):
    columns = []
    for c in range(GROUP):
        start = group * GROUP + c
        columns.append(
            jnp.concatenate(
                [wide[j, pl.ds(start, sources, stride=channels), :] for j in range(3)], axis=0
            )
        )
    return jnp.concatenate(columns, axis=1)


def put_rows(wide, group, sources, channels, rows):
    for c in range(GROUP):
        start = group * GROUP + c
        for j in range(3):
            wide[j, pl.ds(start, sources, stride=channels), :] = rows[
                j * sources : (j + 1) * sources, c * LANES : (c + 1) * LANES
            ]


def forward(stacked, first, twist, middle):
    cos, sin = twist[0], twist[1]
    waves = dot(first, stacked)
    rows = []
    for c in range(GROUP):
        real = waves[:HALF, c * LANES : (c + 1) * LANES]
        imag = waves[HALF:, c * LANES : (c + 1) * LANES]
        rows.append(
            jnp.concatenate([real * cos + imag * sin, imag * cos - real * sin], axis=1)
        )
    return dot(jnp.concatenate(rows, axis=0).astype(BF16), middle)


def inverse(real, imag, back, twist, last):
    cos, sin = twist[0], twist[1]
    turned = dot(jnp.concatenate([real, imag], axis=1).astype(BF16), back)
    columns = []
    for c in range(GROUP):
        zr = turned[c * HALF : (c + 1) * HALF, :LANES]
        zi = turned[c * HALF : (c + 1) * HALF, LANES:]
        columns.append(
            jnp.concatenate([zr * cos - zi * sin, zr * sin + zi * cos], axis=0)
        )
    waves = jnp.concatenate(columns, axis=1).astype(BF16)
    return dot(last, jnp.concatenate([waves, waves], axis=0))


def kernel(
    scale,
    sources,
    channels,
    query_hbm,
    key_hbm,
    value_hbm,
    cotan_hbm,
    taps_hbm,
    first_hbm,
    first_wide_hbm,
    last_hbm,
    middle_hbm,
    back_hbm,
    twist_hbm,
    out_hbm,
    gquery_hbm,
    gkey_hbm,
    gvalue_hbm,
    gfilter_hbm,
    query,
    key,
    value,
    cotan,
    taps,
    first,
    first_wide,
    last,
    middle,
    back,
    twist,
    out_buf,
    gfilter,
    gate_send,
    back_send,
    gate_recv,
    back_recv,
    conv_send,
    bconv_send,
    conv_recv,
    bconv_recv,
    wide_in,
    wide_out,
    filt_spec,
    gate_spec,
    core_send,
    core_recv,
    x_send,
    x_recv,
    z_send,
    z_recv,
    total,
    load_sem,
    store_sem,
    send_sem,
    recv_sem,
    red_send,
    red_recv,
):
    me = lax.axis_index("ctx")
    rep = lax.axis_index("rep")
    zl = rep // 8
    xc = rep // 2 % 4
    core = rep % 2
    tokens = 3 * LANES
    groups = channels // GROUP

    barrier = pltpu.get_barrier_semaphore()

    def greet(step, carry):
        peer = lax.rem(me + step, sources)
        pl.semaphore_signal(barrier, inc=1, device_id=(rep, peer), device_id_type=MESH)
        return carry

    other_core = rep + 1 - 2 * core
    other_z = (1 - zl) * 8 + xc * 2 + core

    def x_peer(step):
        return zl * 8 + lax.rem(xc + step, 4) * 2 + core

    lax.fori_loop(1, sources, greet, 0)
    for peer in [other_core, other_z] + [x_peer(step) for step in range(1, 4)]:
        pl.semaphore_signal(barrier, inc=1, device_id=(peer, me), device_id_type=MESH)

    loads = []
    for index, (src, dst) in enumerate(
        [
            (key_hbm, key),
            (value_hbm, value),
            (cotan_hbm, cotan),
            (query_hbm, query),
            (taps_hbm, taps),
            (first_hbm, first),
            (first_wide_hbm, first_wide),
            (last_hbm, last),
            (middle_hbm, middle),
            (back_hbm, back),
            (twist_hbm, twist),
        ]
    ):
        load = pltpu.make_async_copy(src, dst, load_sem.at[index])
        load.start()
        loads.append(load)

    def products(left, right, held):
        def body(c, carry):
            lane = pl.ds(pl.multiple_of(c * LANES, LANES), LANES)
            for i in range(3):
                spot = pl.ds(i * LANES, LANES)
                both = left[spot, lane].astype(F32) * right[spot, lane].astype(F32)
                held[lane, spot] = both.T.astype(BF16)
            return carry

        lax.fori_loop(0, left.shape[1] // LANES, body, 0)

    def exchange(kind, held, landing):
        def copy(peer, sender):
            return pltpu.make_async_remote_copy(
                src_ref=held.at[pl.ds(peer * channels, channels), :],
                dst_ref=landing.at[sender],
                send_sem=send_sem.at[kind, peer],
                recv_sem=recv_sem.at[kind, sender],
                device_id=(rep, peer),
                device_id_type=MESH,
            )

        def start(step, carry):
            copy(lax.rem(me + step, sources), me).start()
            return carry

        def arrive(step, carry):
            peer = lax.rem(me + step, sources)
            copy(peer, peer).wait_recv()
            return carry

        def leave(step, carry):
            copy(lax.rem(me + step, sources), me).wait_send()
            return carry

        def go():
            lax.fori_loop(1, sources, start, 0)
            landing[me] = held[pl.ds(pl.multiple_of(me * channels, channels), channels), :]

        return (
            go,
            lambda: lax.fori_loop(1, sources, arrive, 0),
            lambda: lax.fori_loop(1, sources, leave, 0),
        )

    gate_go, gate_arrive, gate_leave = exchange(0, gate_send, gate_recv)
    back_go, back_arrive, back_leave = exchange(1, back_send, back_recv)
    conv_go, conv_arrive, conv_leave = exchange(2, conv_send, conv_recv)
    bconv_go, bconv_arrive, bconv_leave = exchange(3, bconv_send, bconv_recv)

    loads[0].wait()
    loads[1].wait()
    products(key, value, gate_send)
    loads[2].wait()
    loads[3].wait()
    products(cotan, query, back_send)

    pl.semaphore_wait(barrier, sources - 1 + 5)
    gate_go()
    back_go()

    loads[4].wait()
    for load in loads[5:]:
        load.wait()

    def turn_taps(s, carry):
        for j in range(3):
            spot = pl.ds(pl.multiple_of((s * 3 + j) * LANES, LANES), LANES)
            wide_in[j, pl.ds(pl.multiple_of(s * channels, channels), channels), :] = taps[spot, :].T
        return carry

    lax.fori_loop(0, sources, turn_taps, 0)

    def filter_group(g, carry):
        rows = take_rows(wide_in, g, sources, channels)
        high = rows.astype(BF16)
        low = (rows - high.astype(F32)).astype(BF16)
        filt_spec[g] = forward(
            jnp.concatenate([high, high, low], axis=0), first_wide[...], twist, middle[...]
        )
        return carry

    lax.fori_loop(0, groups, filter_group, 0)

    def widen(landing):
        def body(s, carry):
            for j in range(3):
                wide_in[j, pl.ds(pl.multiple_of(s * channels, channels), channels), :] = landing[
                    s, :, j * LANES : (j + 1) * LANES
                ].astype(F32)
            return carry

        lax.fori_loop(0, sources, body, 0)

    def narrow(held):
        def body(s, carry):
            spot = pl.ds(pl.multiple_of(s * channels, channels), channels)
            for j in range(3):
                held[spot, j * LANES : (j + 1) * LANES] = wide_out[j, spot, :].astype(BF16)
            return carry

        lax.fori_loop(0, sources, body, 0)

    def spectrum(g):
        rows = take_rows(wide_in, g, sources, channels).astype(BF16)
        return forward(jnp.concatenate([rows, rows], axis=0), first[...], twist, middle[...])

    gate_arrive()
    widen(gate_recv)

    def conv_group(g, carry):
        spec = spectrum(g)
        gate_spec[g] = spec
        gr, gi = spec[:, :LANES], spec[:, LANES:]
        hr, hi = filt_spec[g, :, :LANES], filt_spec[g, :, LANES:]
        rows = inverse(gr * hr - gi * hi, gr * hi + gi * hr, back[...], twist, last[...])
        put_rows(wide_out, g, sources, channels, rows)
        return carry

    lax.fori_loop(0, groups, conv_group, 0)
    narrow(conv_send)
    conv_go()

    back_arrive()
    widen(back_recv)

    def bconv_group(g, carry):
        spec = spectrum(g)
        br, bi = spec[:, :LANES], spec[:, LANES:]
        hr, hi = filt_spec[g, :, :LANES], filt_spec[g, :, LANES:]
        rows = inverse(br * hr + bi * hi, bi * hr - br * hi, back[...], twist, last[...])
        put_rows(wide_out, g, sources, channels, rows)
        gr, gi = gate_spec[g, :, :LANES], gate_spec[g, :, LANES:]
        gate_spec[g] = jnp.concatenate([br * gr + bi * gi, bi * gr - br * gi], axis=1)
        return carry

    lax.fori_loop(0, groups, bconv_group, 0)
    narrow(bconv_send)
    bconv_go()

    def term_group(g, carry):
        rows = inverse(
            gate_spec[g, :, :LANES], gate_spec[g, :, LANES:], back[...], twist, last[...]
        )
        put_rows(wide_out, g, sources, channels, rows)
        return carry

    lax.fori_loop(0, groups, term_group, 0)

    def term_rows(where):
        spot = pl.ds(pl.multiple_of(where * channels, channels), channels)
        return [wide_out[j, spot, :] for j in range(3)]

    def fill_core(i, carry):
        where = i % 2 * 8 + i // 2 * 2 + 1 - core
        for j, rows in enumerate(term_rows(where)):
            core_send[i, :, j * LANES : (j + 1) * LANES] = rows.astype(BF16)
        return carry

    lax.fori_loop(0, 8, fill_core, 0)
    core_copy = pltpu.make_async_remote_copy(
        src_ref=core_send,
        dst_ref=core_recv,
        send_sem=red_send.at[0],
        recv_sem=red_recv.at[0],
        device_id=(other_core, me),
        device_id_type=MESH,
    )
    core_copy.start()

    def results(landing, parts):
        def body(c, carry):
            lane = pl.ds(pl.multiple_of(c * LANES, LANES), LANES)
            for i in range(3):
                spot = pl.ds(i * LANES, LANES)
                block = landing[pl.ds(c * 4, 4), :, i * LANES : (i + 1) * LANES]
                rows = block.reshape(LANES, LANES).astype(F32).T
                for other, held in parts:
                    held[spot, lane] = (other[spot, lane].astype(F32) * rows).astype(BF16)
            return carry

        lax.fori_loop(0, query.shape[1] // LANES, body, 0)

    def store(index, src, dst):
        copy = pltpu.make_async_copy(src, dst, store_sem.at[index])
        copy.start()
        return copy

    conv_arrive()
    results(conv_recv, [(query, out_buf.at[0]), (cotan, out_buf.at[1])])
    stores = [store(0, out_buf.at[0], out_hbm), store(1, out_buf.at[1], gquery_hbm)]

    core_copy.wait()

    def add_core(i, carry):
        where = i % 2 * 8 + i // 2 * 2 + core
        for j, rows in enumerate(term_rows(where)):
            lane = slice(j * LANES, (j + 1) * LANES)
            added = rows + core_recv[i, :, lane].astype(F32)
            total[i, :, lane] = added
            x_send[i, :, lane] = added.astype(BF16)
        return carry

    lax.fori_loop(0, 8, add_core, 0)
    x_copies = []
    for step in range(1, 4):
        there = lax.rem(xc + step, 4)
        copy = pltpu.make_async_remote_copy(
            src_ref=x_send.at[pl.ds(there * 2, 2)],
            dst_ref=x_recv.at[step - 1],
            send_sem=red_send.at[step],
            recv_sem=red_recv.at[step],
            device_id=(x_peer(step), me),
            device_id_type=MESH,
        )
        copy.start()
        x_copies.append(copy)
    for copy in x_copies:
        copy.wait()

    def x_sum(which):
        added = total[xc * 2 + which]
        for step in range(3):
            added = added + x_recv[step, which].astype(F32)
        return added

    z_send[...] = x_sum(1 - zl).astype(BF16)
    z_copy = pltpu.make_async_remote_copy(
        src_ref=z_send,
        dst_ref=z_recv,
        send_sem=red_send.at[4],
        recv_sem=red_recv.at[4],
        device_id=(other_z, me),
        device_id_type=MESH,
    )
    z_copy.start()
    own = x_sum(zl)
    z_copy.wait()
    summed = (own + z_recv[...].astype(F32)) * scale
    for j in range(3):
        gfilter[j * LANES : (j + 1) * LANES, :] = summed[:, j * LANES : (j + 1) * LANES].T
    stores.append(store(4, gfilter, gfilter_hbm))

    bconv_arrive()
    results(bconv_recv, [(value, out_buf.at[2]), (key, out_buf.at[3])])
    stores += [store(2, out_buf.at[2], gkey_hbm), store(3, out_buf.at[3], gvalue_hbm)]
    gate_leave()
    back_leave()
    conv_leave()
    bconv_leave()
    for copy in stores:
        copy.wait()


def on_device(tables, query_feat, key_feat, value_feat, filter_taps, out_cotangent):
    tokens, width = query_feat.shape[1:]
    sources = lax.axis_size("ctx")
    channels = width // sources
    groups = channels // GROUP
    scale = 1.0 / math.sqrt(lax.axis_size("rep") * tokens * sources)
    seq = jax.ShapeDtypeStruct((tokens, width), BF16)
    anywhere = pl.BlockSpec(memory_space=pl.ANY)
    block = (sources, channels, tokens)
    vmem = pltpu.VMEM
    outs = pl.pallas_call(
        functools.partial(kernel, scale, sources, channels),
        out_shape=(seq, seq, seq, seq, jax.ShapeDtypeStruct((tokens, channels), F32)),
        in_specs=[anywhere] * (5 + len(tables)),
        out_specs=(anywhere,) * 5,
        scratch_shapes=[
            vmem((tokens, width), BF16),
            vmem((tokens, width), BF16),
            vmem((tokens, width), BF16),
            vmem((tokens, width), BF16),
            vmem(filter_taps.shape, F32),
            *[vmem(table.shape, table.dtype) for table in tables],
            vmem((4, tokens, width), BF16),
            vmem((tokens, channels), F32),
            vmem((width, tokens), BF16),
            vmem((width, tokens), BF16),
            vmem(block, BF16),
            vmem(block, BF16),
            vmem((width, tokens), BF16),
            vmem((width, tokens), BF16),
            vmem(block, BF16),
            vmem(block, BF16),
            vmem((3, sources * channels, LANES), F32),
            vmem((3, sources * channels, LANES), F32),
            vmem((groups, GROUP * HALF, 2 * LANES), F32),
            vmem((groups, GROUP * HALF, 2 * LANES), F32),
            vmem((8, channels, tokens), BF16),
            vmem((8, channels, tokens), BF16),
            vmem((8, channels, tokens), BF16),
            vmem((3, 2, channels, tokens), BF16),
            vmem((channels, tokens), BF16),
            vmem((channels, tokens), BF16),
            vmem((8, channels, tokens), F32),
            pltpu.SemaphoreType.DMA((5 + len(tables),)),
            pltpu.SemaphoreType.DMA((5,)),
            pltpu.SemaphoreType.DMA((4, sources)),
            pltpu.SemaphoreType.DMA((4, sources)),
            pltpu.SemaphoreType.DMA((5,)),
            pltpu.SemaphoreType.DMA((5,)),
        ],
        compiler_params=pltpu.CompilerParams(
            collective_id=0, has_side_effects=True, vmem_limit_bytes=48 * 2**20
        ),
    )(
        query_feat[0],
        key_feat[0],
        value_feat[0],
        out_cotangent[0],
        filter_taps,
        *[jnp.asarray(table) for table in tables],
    )
    return (*[out[None] for out in outs[:4]], outs[4])


def solution(mesh):
    tables = wave_tables(mesh.shape["ctx"])
    rows = P("rep", "ctx", None)
    return jax.shard_map(
        functools.partial(on_device, tables),
        mesh=mesh,
        in_specs=(rows, rows, rows, P(None, "ctx"), rows),
        out_specs=(rows, rows, rows, rows, P("rep", "ctx")),
        check_vma=False,
    )
```

profile of v0, /device:TPU:56, one launch (start us, length us, event | category | flops | bytes accessed | tf_op | source)
XLA Modules:
  0.0 63.3 jit_solution(15030393637604798941)
XLA Ops:
  0.6 0.0 copy-start.6
  0.6 0.0 copy-start.4
  0.7 0.0 copy-start.9
  0.7 0.0 copy-start.3
  0.7 0.0 copy-start.2
  0.7 0.0 copy-start.1
  0.7 0.0 copy-start
  0.7 3.2 %copy.16.taps_hbm = f32[6144,32]{1,0:T(8,128)} copy(f32[6144,32]{0,1:T(8,128)} %param.14) | data formatting | bytes 1572864 | tf_op args[3]
  3.9 0.0 copy-done.6
  4.0 0.0 copy-done.4
  4.0 0.0 copy-done.9
  4.0 0.0 copy-done.3
  4.0 0.0 copy-done.2
  4.0 0.0 copy-done.1
  4.0 0.0 copy-done
  4.0 0.0 copy-start.5
  4.0 0.9 %copy-done.5 = bf16[256,256]{1,0:T(8,128)(2,1)S(1)} copy-done((bf16[256,256]{1,0:T(8,128)(2,1)S(1)}, bf16[256,256]{1,0:T(8,128)(2,1)}, u32[]{:S(2)}) %copy-start.5) | copy-done | bytes 131096
  4.9 0.0 copy-start.7
  4.9 0.8 %copy-done.7 = bf16[112,144]{1,0:T(8,128)(2,1)S(1)} copy-done((bf16[112,144]{1,0:T(8,128)(2,1)S(1)}, bf16[112,144]{1,0:T(8,128)(2,1)}, u32[]{:S(2)}) %copy-start.7) | copy-done | bytes 32280
  5.7 0.0 copy-start.8
  5.7 0.7 %copy-done.8 = bf16[112,96]{1,0:T(8,128)(2,1)S(1)} copy-done((bf16[112,96]{1,0:T(8,128)(2,1)S(1)}, bf16[112,96]{1,0:T(8,128)(2,1)}, u32[]{:S(2)}) %copy-start.8) | copy-done | bytes 21528
  6.5 53.1 %shard_map.146 = (bf16[384,512]{1,0:T(8,128)(2,1)S(1)}, bf16[384,512]{1,0:T(8,128)(2,1)S(1)}, bf16[384,512]{1,0:T(8,128)(2,1)S(1)}, bf16[384,512]{1,0:T(8,128)(2,1)S(1)}, f32[384,32]{1,0:T(8,128)S(1)}) custom-call(bf16[384,512]{1,0:T(8,128)(2,1)S(1)} %bitcast.8, bf16[384,512]{1,0:T(8,128)(2,1)S(1)} %bitcast.9, bf16[384,512]{1,0:T(8,128)(2,1)S(1)} %bitcast.10, ...), custom_call_target="tpu_custom_call" | custom-call | tf_op jit(solution)/shard_map/pallas_call | solution.py:488
  59.6 0.7 %copy.17 = f32[384,32]{0,1:T(8,128)} copy(f32[384,32]{1,0:T(8,128)S(1)} %get-tuple-element.19) | data formatting | bytes 98304
  60.3 0.7 %copy.22 = bf16[1,384,512]{2,1,0:T(8,128)(2,1)} copy(bf16[1,384,512]{2,1,0:T(8,128)(2,1)S(1)} %bitcast.15) | data formatting | bytes 786432
  61.1 0.7 %copy.23 = bf16[1,384,512]{2,1,0:T(8,128)(2,1)} copy(bf16[1,384,512]{2,1,0:T(8,128)(2,1)S(1)} %bitcast.14) | data formatting | bytes 786432
  61.8 0.7 %copy.24 = bf16[1,384,512]{2,1,0:T(8,128)(2,1)} copy(bf16[1,384,512]{2,1,0:T(8,128)(2,1)S(1)} %bitcast.13) | data formatting | bytes 786432
  62.6 0.7 %copy.25 = bf16[1,384,512]{2,1,0:T(8,128)(2,1)} copy(bf16[1,384,512]{2,1,0:T(8,128)(2,1)S(1)} %bitcast.12) | data formatting | bytes 786432
Async XLA Ops:
  0.6 3.3 %copy-start.6 = (f32[2,56,128]{2,1,0:T(8,128)S(1)}, f32[2,56,128]{2,1,0:T(8,128)}, u32[]{:S(2)}) copy-start(f32[2,56,128]{2,1,0:T(8,128)} %constant.17.clone.twist_hbm) | copy-start | bytes 172036
  0.6 3.3 %copy-start.4 = (bf16[256,256]{1,0:T(8,128)(2,1)S(1)}, bf16[256,256]{1,0:T(8,128)(2,1)}, u32[]{:S(2)}) copy-start(bf16[256,256]{1,0:T(8,128)(2,1)} %constant.16.clone.back_hbm) | copy-start | bytes 393220
  0.7 3.3 %copy-start.9 = (bf16[48,224]{1,0:T(8,128)(2,1)S(1)}, bf16[48,224]{1,0:T(8,128)(2,1)}, u32[]{:S(2)}) copy-start(bf16[48,224]{1,0:T(8,128)(2,1)} %constant.14.clone.last_hbm) | copy-start | bytes 64516
  0.7 3.3 %copy-start.3 = (bf16[1,384,512]{2,1,0:T(8,128)(2,1)S(1)}, bf16[1,384,512]{2,1,0:T(8,128)(2,1)}, u32[]{:S(2)}) copy-start(bf16[1,384,512]{2,1,0:T(8,128)(2,1)} %param.15) | copy-start | bytes 1179652
  0.7 3.3 %copy-start.2 = (bf16[1,384,512]{2,1,0:T(8,128)(2,1)S(1)}, bf16[1,384,512]{2,1,0:T(8,128)(2,1)}, u32[]{:S(2)}) copy-start(bf16[1,384,512]{2,1,0:T(8,128)(2,1)} %param.13) | copy-start | bytes 1179652
  0.7 3.3 %copy-start.1 = (bf16[1,384,512]{2,1,0:T(8,128)(2,1)S(1)}, bf16[1,384,512]{2,1,0:T(8,128)(2,1)}, u32[]{:S(2)}) copy-start(bf16[1,384,512]{2,1,0:T(8,128)(2,1)} %param.12) | copy-start | bytes 1179652
  0.7 3.3 %copy-start = (bf16[1,384,512]{2,1,0:T(8,128)(2,1)S(1)}, bf16[1,384,512]{2,1,0:T(8,128)(2,1)}, u32[]{:S(2)}) copy-start(bf16[1,384,512]{2,1,0:T(8,128)(2,1)} %param.11) | copy-start | bytes 1179652
  4.0 0.9 %copy-start.5 = (bf16[256,256]{1,0:T(8,128)(2,1)S(1)}, bf16[256,256]{1,0:T(8,128)(2,1)}, u32[]{:S(2)}) copy-start(bf16[256,256]{1,0:T(8,128)(2,1)} %constant.15.clone.middle_hbm) | copy-start | bytes 393220
  4.9 0.8 %copy-start.7 = (bf16[112,144]{1,0:T(8,128)(2,1)S(1)}, bf16[112,144]{1,0:T(8,128)(2,1)}, u32[]{:S(2)}) copy-start(bf16[112,144]{1,0:T(8,128)(2,1)} %constant.13.clone.first_wide_hbm) | copy-start | bytes 96772
  5.7 0.7 %copy-start.8 = (bf16[112,96]{1,0:T(8,128)(2,1)S(1)}, bf16[112,96]{1,0:T(8,128)(2,1)}, u32[]{:S(2)}) copy-start(bf16[112,96]{1,0:T(8,128)(2,1)} %constant.12.clone.first_hbm) | copy-start | bytes 64516
where the time goes:
time: 63.6 us; the launch traced here: 63.3 us
  Pallas kernels  53.1 us (83%)
  local copies, waits for them, and re-layouts  9.45 us (15%)
  between operations  0.74 us (1%)
    pallas_call x1, Pallas kernels, on_device(): pl.pallas_call(functools.partial(kernel, scale, sources, channels), out_s...  53.1 us
    unnamed x26, local copies, waits for them, and re-layouts  9.45 us

commit v1 on v0

--- a/solution.py
+++ b/solution.py
@@ -55,13 +55,16 @@
 
     first_high, first_low = split_table(first)
     last_high, last_low = split_table(last)
-    return (
-        np.concatenate([first_high, first_low], axis=1),
+    parts = (
         np.concatenate([first_high, first_low, first_high], axis=1),
         np.concatenate([last_high, last_low], axis=1),
-        middle.astype(ml_dtypes.bfloat16),
-        back.astype(ml_dtypes.bfloat16),
-        twist.astype(np.float32),
+        middle,
+        back,
+        np.concatenate([twist[0], twist[1]], axis=1),
+    )
+    width = 2 * LANES
+    return np.concatenate(
+        [np.pad(part.astype(np.float32), ((0, 0), (0, width - part.shape[1]))) for part in parts]
     )
 
 
@@ -126,38 +129,27 @@
     value_hbm,
     cotan_hbm,
     taps_hbm,
-    first_hbm,
-    first_wide_hbm,
-    last_hbm,
-    middle_hbm,
-    back_hbm,
-    twist_hbm,
-    out_hbm,
-    gquery_hbm,
-    gkey_hbm,
-    gvalue_hbm,
-    gfilter_hbm,
+    tables_hbm,
+    conv_recv,
+    bconv_recv,
+    gfilter,
     query,
     key,
     value,
     cotan,
     taps,
+    tables,
     first,
-    first_wide,
     last,
     middle,
     back,
     twist,
-    out_buf,
-    gfilter,
     gate_send,
     back_send,
     gate_recv,
     back_recv,
     conv_send,
     bconv_send,
-    conv_recv,
-    bconv_recv,
     wide_in,
     wide_out,
     filt_spec,
@@ -170,7 +162,7 @@
     z_recv,
     total,
     load_sem,
-    store_sem,
+    own_sem,
     send_sem,
     recv_sem,
     red_send,
@@ -209,12 +201,7 @@
             (cotan_hbm, cotan),
             (query_hbm, query),
             (taps_hbm, taps),
-            (first_hbm, first),
-            (first_wide_hbm, first_wide),
-            (last_hbm, last),
-            (middle_hbm, middle),
-            (back_hbm, back),
-            (twist_hbm, twist),
+            (tables_hbm, tables),
         ]
     ):
         load = pltpu.make_async_copy(src, dst, load_sem.at[index])
@@ -231,6 +218,13 @@
             return carry
 
         lax.fori_loop(0, left.shape[1] // LANES, body, 0)
+
+    def own(kind, held, landing):
+        return pltpu.make_async_copy(
+            held.at[pl.ds(pl.multiple_of(me * channels, channels), channels), :],
+            landing.at[me],
+            own_sem.at[kind],
+        )
 
     def exchange(kind, held, landing):
         def copy(peer, sender):
@@ -258,11 +252,15 @@
 
         def go():
             lax.fori_loop(1, sources, start, 0)
-            landing[me] = held[pl.ds(pl.multiple_of(me * channels, channels), channels), :]
+            own(kind, held, landing).start()
+
+        def arrive_all():
+            own(kind, held, landing).wait()
+            lax.fori_loop(1, sources, arrive, 0)
 
         return (
             go,
-            lambda: lax.fori_loop(1, sources, arrive, 0),
+            arrive_all,
             lambda: lax.fori_loop(1, sources, leave, 0),
         )
 
@@ -274,22 +272,30 @@
     loads[0].wait()
     loads[1].wait()
     products(key, value, gate_send)
+    with jax.named_scope("barrier"):
+        pl.semaphore_wait(barrier, sources - 1 + 5)
+    with jax.named_scope("gate_go"):
+        gate_go()
     loads[2].wait()
     loads[3].wait()
-    products(cotan, query, back_send)
-
-    pl.semaphore_wait(barrier, sources - 1 + 5)
-    gate_go()
-    back_go()
+    with jax.named_scope("back_products"):
+        products(cotan, query, back_send)
+    with jax.named_scope("back_go"):
+        back_go()
 
     loads[4].wait()
-    for load in loads[5:]:
-        load.wait()
+    loads[5].wait()
+    rows = 0
+    for held in (first, last, middle, back):
+        held[...] = tables[rows : rows + held.shape[0], : held.shape[1]].astype(BF16)
+        rows += held.shape[0]
+    for part in range(2):
+        twist[part] = tables[rows : rows + HALF, part * LANES : (part + 1) * LANES]
 
     def turn_taps(s, carry):
         for j in range(3):
             spot = pl.ds(pl.multiple_of((s * 3 + j) * LANES, LANES), LANES)
-            wide_in[j, pl.ds(pl.multiple_of(s * channels, channels), channels), :] = taps[spot, :].T
+            wide_in[j, pl.ds(pl.multiple_of(s * channels, channels), channels), :] = taps[:, spot]
         return carry
 
     lax.fori_loop(0, sources, turn_taps, 0)
@@ -299,7 +305,7 @@
         high = rows.astype(BF16)
         low = (rows - high.astype(F32)).astype(BF16)
         filt_spec[g] = forward(
-            jnp.concatenate([high, high, low], axis=0), first_wide[...], twist, middle[...]
+            jnp.concatenate([high, high, low], axis=0), first[...], twist, middle[...]
         )
         return carry
 
@@ -326,7 +332,7 @@
 
     def spectrum(g):
         rows = take_rows(wide_in, g, sources, channels).astype(BF16)
-        return forward(jnp.concatenate([rows, rows], axis=0), first[...], twist, middle[...])
+        return forward(jnp.concatenate([rows, rows], axis=0), first[:, : 2 * sources * 3], twist, middle[...])
 
     gate_arrive()
     widen(gate_recv)
@@ -390,28 +396,6 @@
         device_id_type=MESH,
     )
     core_copy.start()
-
-    def results(landing, parts):
-        def body(c, carry):
-            lane = pl.ds(pl.multiple_of(c * LANES, LANES), LANES)
-            for i in range(3):
-                spot = pl.ds(i * LANES, LANES)
-                block = landing[pl.ds(c * 4, 4), :, i * LANES : (i + 1) * LANES]
-                rows = block.reshape(LANES, LANES).astype(F32).T
-                for other, held in parts:
-                    held[spot, lane] = (other[spot, lane].astype(F32) * rows).astype(BF16)
-            return carry
-
-        lax.fori_loop(0, query.shape[1] // LANES, body, 0)
-
-    def store(index, src, dst):
-        copy = pltpu.make_async_copy(src, dst, store_sem.at[index])
-        copy.start()
-        return copy
-
-    conv_arrive()
-    results(conv_recv, [(query, out_buf.at[0]), (cotan, out_buf.at[1])])
-    stores = [store(0, out_buf.at[0], out_hbm), store(1, out_buf.at[1], gquery_hbm)]
 
     core_copy.wait()
 
@@ -457,20 +441,84 @@
         device_id_type=MESH,
     )
     z_copy.start()
-    own = x_sum(zl)
+    mine = x_sum(zl)
     z_copy.wait()
-    summed = (own + z_recv[...].astype(F32)) * scale
-    for j in range(3):
-        gfilter[j * LANES : (j + 1) * LANES, :] = summed[:, j * LANES : (j + 1) * LANES].T
-    stores.append(store(4, gfilter, gfilter_hbm))
-
+    summed = (mine + z_recv[...].astype(F32)) * scale
+    gfilter[...] = summed
+
+    conv_arrive()
     bconv_arrive()
-    results(bconv_recv, [(value, out_buf.at[2]), (key, out_buf.at[3])])
-    stores += [store(2, out_buf.at[2], gkey_hbm), store(3, out_buf.at[3], gvalue_hbm)]
     gate_leave()
     back_leave()
     conv_leave()
     bconv_leave()
+
+
+def finish(
+    conv_hbm,
+    bconv_hbm,
+    term_hbm,
+    query_hbm,
+    key_hbm,
+    value_hbm,
+    cotan_hbm,
+    out_hbm,
+    gquery_hbm,
+    gkey_hbm,
+    gvalue_hbm,
+    gfilter_hbm,
+    conv,
+    bconv,
+    term,
+    query,
+    key,
+    value,
+    cotan,
+    out_buf,
+    load_sem,
+    store_sem,
+):
+    loads = []
+    for index, (src, dst) in enumerate(
+        [
+            (bconv_hbm, bconv),
+            (key_hbm, key),
+            (value_hbm, value),
+            (conv_hbm, conv),
+            (query_hbm, query),
+            (cotan_hbm, cotan),
+            (term_hbm, term),
+        ]
+    ):
+        load = pltpu.make_async_copy(src, dst, load_sem.at[index])
+        load.start()
+        loads.append(load)
+    stores = []
+
+    def results(landing, parts):
+        for c in range(query.shape[1] // LANES):
+            lane = slice(c * LANES, (c + 1) * LANES)
+            for i in range(3):
+                spot = slice(i * LANES, (i + 1) * LANES)
+                rows = landing[lane, spot].astype(F32).T
+                for which, other, dst in parts:
+                    out_buf[which, spot, lane] = (other[spot, lane].astype(F32) * rows).astype(BF16)
+            for which, other, dst in parts:
+                copy = pltpu.make_async_copy(
+                    out_buf.at[which, :, lane], dst.at[:, lane], store_sem.at[which, c]
+                )
+                copy.start()
+                stores.append(copy)
+
+    for load in loads[:3]:
+        load.wait()
+    results(bconv, [(2, value, gkey_hbm), (3, key, gvalue_hbm)])
+    for load in loads[3:]:
+        load.wait()
+    copy = pltpu.make_async_copy(term, gfilter_hbm, load_sem.at[0])
+    copy.start()
+    stores.append(copy)
+    results(conv, [(0, query, out_hbm), (1, cotan, gquery_hbm)])
     for copy in stores:
         copy.wait()
 
@@ -480,33 +528,33 @@
     sources = lax.axis_size("ctx")
     channels = width // sources
     groups = channels // GROUP
+    rows = sources * 3
     scale = 1.0 / math.sqrt(lax.axis_size("rep") * tokens * sources)
-    seq = jax.ShapeDtypeStruct((tokens, width), BF16)
     anywhere = pl.BlockSpec(memory_space=pl.ANY)
     block = (sources, channels, tokens)
+    landing = jax.ShapeDtypeStruct(block, BF16)
     vmem = pltpu.VMEM
-    outs = pl.pallas_call(
+    features = (query_feat[0], key_feat[0], value_feat[0], out_cotangent[0])
+    conv, bconv, term = pl.pallas_call(
         functools.partial(kernel, scale, sources, channels),
-        out_shape=(seq, seq, seq, seq, jax.ShapeDtypeStruct((tokens, channels), F32)),
-        in_specs=[anywhere] * (5 + len(tables)),
-        out_specs=(anywhere,) * 5,
+        out_shape=(landing, landing, jax.ShapeDtypeStruct((channels, tokens), F32)),
+        in_specs=[pl.BlockSpec(memory_space=pltpu.HBM)] * 6,
+        out_specs=(anywhere, anywhere, pl.BlockSpec(memory_space=pltpu.VMEM)),
         scratch_shapes=[
-            vmem((tokens, width), BF16),
-            vmem((tokens, width), BF16),
-            vmem((tokens, width), BF16),
-            vmem((tokens, width), BF16),
-            vmem(filter_taps.shape, F32),
-            *[vmem(table.shape, table.dtype) for table in tables],
-            vmem((4, tokens, width), BF16),
-            vmem((tokens, channels), F32),
+            *[vmem((tokens, width), BF16)] * 4,
+            vmem(filter_taps.shape[::-1], F32),
+            vmem(tables.shape, F32),
+            vmem((2 * HALF, 3 * rows), BF16),
+            vmem((rows, 4 * HALF), BF16),
+            vmem((2 * LANES, 2 * LANES), BF16),
+            vmem((2 * LANES, 2 * LANES), BF16),
+            vmem((2, HALF, LANES), F32),
             vmem((width, tokens), BF16),
             vmem((width, tokens), BF16),
             vmem(block, BF16),
             vmem(block, BF16),
             vmem((width, tokens), BF16),
             vmem((width, tokens), BF16),
-            vmem(block, BF16),
-            vmem(block, BF16),
             vmem((3, sources * channels, LANES), F32),
             vmem((3, sources * channels, LANES), F32),
             vmem((groups, GROUP * HALF, 2 * LANES), F32),
@@ -518,25 +566,35 @@
             vmem((channels, tokens), BF16),
             vmem((channels, tokens), BF16),
             vmem((8, channels, tokens), F32),
-            pltpu.SemaphoreType.DMA((5 + len(tables),)),
-            pltpu.SemaphoreType.DMA((5,)),
+            pltpu.SemaphoreType.DMA((6,)),
+            pltpu.SemaphoreType.DMA((4,)),
             pltpu.SemaphoreType.DMA((4, sources)),
             pltpu.SemaphoreType.DMA((4, sources)),
             pltpu.SemaphoreType.DMA((5,)),
             pltpu.SemaphoreType.DMA((5,)),
         ],
         compiler_params=pltpu.CompilerParams(
-            collective_id=0, has_side_effects=True, vmem_limit_bytes=48 * 2**20
+            collective_id=0, has_side_effects=True, vmem_limit_bytes=60 * 2**20
         ),
-    )(
-        query_feat[0],
-        key_feat[0],
-        value_feat[0],
-        out_cotangent[0],
-        filter_taps,
-        *[jnp.asarray(table) for table in tables],
-    )
-    return (*[out[None] for out in outs[:4]], outs[4])
+    )(*features, filter_taps.T, jnp.asarray(tables))
+    seq = jax.ShapeDtypeStruct((tokens, width), BF16)
+    outs = pl.pallas_call(
+        finish,
+        out_shape=(seq, seq, seq, seq, jax.ShapeDtypeStruct((channels, tokens), F32)),
+        in_specs=[anywhere] * 7,
+        out_specs=(anywhere,) * 5,
+        scratch_shapes=[
+            vmem((width, tokens), BF16),
+            vmem((width, tokens), BF16),
+            vmem((channels, tokens), F32),
+            *[vmem((tokens, width), BF16)] * 4,
+            vmem((4, tokens, width), BF16),
+            pltpu.SemaphoreType.DMA((7,)),
+            pltpu.SemaphoreType.DMA((4, width // LANES)),
+        ],
+        compiler_params=pltpu.CompilerParams(vmem_limit_bytes=60 * 2**20),
+    )(conv.reshape(width, tokens), bconv.reshape(width, tokens), term, *features)
+    return (*[out[None] for out in outs[:4]], outs[4].T)
 
 
 def solution(mesh):

time: 63.6 us -> 54.8 us (0.86)
  the two profiles are of different devices: /device:TPU:56 before, /device:TPU:24 now
where the time goes in v1:
time: 54.8 us; the launch traced here: 54.7 us
  Pallas kernels  54.1 us (99%)
  between operations  0.64 us (1%)
    pallas_call x1, Pallas kernels, on_device(): pl.pallas_call(functools.partial(kernel, scale, sources, channels), out_s...  51.3 us
    pallas_call x1, Pallas kernels, on_device(): pl.pallas_call(finish, out_shape=(seq, seq, seq, seq, jax.ShapeDtypeStruc...  2.8 us

profile of v1, /device:TPU:24, one launch (start us, length us, event | category | flops | bytes accessed | tf_op | source)
XLA Modules:
  0.0 54.7 jit_solution(7651408010138381038)
XLA Ops:
  0.6 51.3 %shard_map.101 = (bf16[16,32,384]{2,1,0:T(8,128)(2,1)}, bf16[16,32,384]{2,1,0:T(8,128)(2,1)}, f32[32,384]{1,0:T(8,128)}) custom-call(bf16[384,512]{1,0:T(8,128)(2,1)} %bitcast.12, bf16[384,512]{1,0:T(8,128)(2,1)} %bitcast.14, bf16[384,512]{1,0:T(8,128)(2,1)} %bitcast.16, bf16[384,512]{1,0:T(8,128)(2,1)} %bitcast.18, f32[32,6144]{1,0:T(8,128)} %bitcast.20, ...), custom_call_target="tpu_custom_call" | custom-call | tf_op jit(solution)/shard_map/pallas_call | solution.py:538
  51.9 2.8 %shard_map.102 = (bf16[384,512]{1,0:T(8,128)(2,1)}, bf16[384,512]{1,0:T(8,128)(2,1)}, bf16[384,512]{1,0:T(8,128)(2,1)}, bf16[384,512]{1,0:T(8,128)(2,1)}, f32[32,384]{1,0:T(8,128)}) custom-call(bf16[512,384]{1,0:T(8,128)(2,1)} %bitcast.21, bf16[512,384]{1,0:T(8,128)(2,1)} %bitcast.22, f32[32,384]{1,0:T(8,128)} %get-tuple-element.15.term_hbm, ...), custom_call_target="tpu_custom_call" | custom-call | tf_op jit(solution)/shard_map/pallas_call | solution.py:581

commit v2 on v1

--- a/solution.py
+++ b/solution.py
@@ -15,7 +15,7 @@
 BF16 = jnp.bfloat16
 LANES = 128
 HALF = 56
-GROUP = 4
+GROUP = 16
 
 
 def split_table(table):
@@ -130,8 +130,10 @@
     cotan_hbm,
     taps_hbm,
     tables_hbm,
-    conv_recv,
-    bconv_recv,
+    out,
+    gquery,
+    gkey,
+    gvalue,
     gfilter,
     query,
     key,
@@ -150,6 +152,8 @@
     back_recv,
     conv_send,
     bconv_send,
+    conv_recv,
+    bconv_recv,
     wide_in,
     wide_out,
     filt_spec,
@@ -165,11 +169,14 @@
     own_sem,
     send_sem,
     recv_sem,
+    last_sem,
     red_send,
     red_recv,
 ):
     me = lax.axis_index("ctx")
     rep = lax.axis_index("rep")
+    rows_of = sources // 4
+    z, y = me // rows_of, me % rows_of
     zl = rep // 8
     xc = rep // 2 % 4
     core = rep % 2
@@ -219,55 +226,78 @@
 
         lax.fori_loop(0, left.shape[1] // LANES, body, 0)
 
+    far_first = (2, 1, 3, 0)
+
     def own(kind, held, landing):
         return pltpu.make_async_copy(
             held.at[pl.ds(pl.multiple_of(me * channels, channels), channels), :],
-            landing.at[me],
+            landing.at[pl.ds(pl.multiple_of(me * channels, channels), channels), :],
             own_sem.at[kind],
         )
 
+    def copies(kind, held, landing, count, peer, block, incoming):
+        return pltpu.make_async_remote_copy(
+            src_ref=held.at[pl.ds(block * channels, count * channels), :],
+            dst_ref=landing.at[pl.ds(incoming * channels, count * channels), :],
+            send_sem=send_sem.at[kind],
+            recv_sem=recv_sem.at[kind],
+            device_id=(rep, peer),
+            device_id_type=MESH,
+        )
+
     def exchange(kind, held, landing):
-        def copy(peer, sender):
-            return pltpu.make_async_remote_copy(
-                src_ref=held.at[pl.ds(peer * channels, channels), :],
-                dst_ref=landing.at[sender],
-                send_sem=send_sem.at[kind, peer],
-                recv_sem=recv_sem.at[kind, sender],
-                device_id=(rep, peer),
-                device_id_type=MESH,
-            )
-
-        def start(step, carry):
-            copy(lax.rem(me + step, sources), me).start()
-            return carry
-
-        def arrive(step, carry):
-            peer = lax.rem(me + step, sources)
-            copy(peer, peer).wait_recv()
-            return carry
-
-        def leave(step, carry):
-            copy(lax.rem(me + step, sources), me).wait_send()
-            return carry
-
         def go():
-            lax.fori_loop(1, sources, start, 0)
             own(kind, held, landing).start()
-
-        def arrive_all():
+            for dz in far_first:
+
+                def start(step, carry):
+                    peer = lax.rem(z + dz, 4) * rows_of + lax.rem(y + step, rows_of)
+                    copies(kind, held, landing, 1, peer, peer, me).start()
+                    return carry
+
+                lax.fori_loop(0 if dz else 1, rows_of, start, 0)
+
+        def whole():
+            return copies(kind, held, landing, sources - 1, lax.rem(me + 1, sources), 0, 0)
+
+        def arrive():
             own(kind, held, landing).wait()
-            lax.fori_loop(1, sources, arrive, 0)
-
-        return (
-            go,
-            arrive_all,
-            lambda: lax.fori_loop(1, sources, leave, 0),
-        )
+            whole().wait_recv()
+
+        return go, arrive, lambda: whole().wait_send()
 
     gate_go, gate_arrive, gate_leave = exchange(0, gate_send, gate_recv)
     back_go, back_arrive, back_leave = exchange(1, back_send, back_recv)
     conv_go, conv_arrive, conv_leave = exchange(2, conv_send, conv_recv)
-    bconv_go, bconv_arrive, bconv_leave = exchange(3, bconv_send, bconv_recv)
+
+    def last_copy(count, dz, peer, block, incoming):
+        return pltpu.make_async_remote_copy(
+            src_ref=bconv_send.at[pl.ds(block * channels, count * channels), :],
+            dst_ref=bconv_recv.at[pl.ds(incoming * channels, count * channels), :],
+            send_sem=send_sem.at[3],
+            recv_sem=last_sem.at[dz],
+            device_id=(rep, peer),
+            device_id_type=MESH,
+        )
+
+    def bconv_go():
+        own(3, bconv_send, bconv_recv).start()
+        for dz in far_first:
+
+            def start(step, carry):
+                peer = lax.rem(z + dz, 4) * rows_of + lax.rem(y + step, rows_of)
+                last_copy(1, dz, peer, peer, me).start()
+                return carry
+
+            lax.fori_loop(0 if dz else 1, rows_of, start, 0)
+
+    def bconv_arrive(dz):
+        if dz == 0:
+            own(3, bconv_send, bconv_recv).wait()
+        last_copy(rows_of - (dz == 0), dz, lax.rem(me + 1, sources), 0, 0).wait_recv()
+
+    def bconv_leave():
+        last_copy(sources - 1, 0, lax.rem(me + 1, sources), 0, 0).wait_send()
 
     loads[0].wait()
     loads[1].wait()
@@ -314,9 +344,8 @@
     def widen(landing):
         def body(s, carry):
             for j in range(3):
-                wide_in[j, pl.ds(pl.multiple_of(s * channels, channels), channels), :] = landing[
-                    s, :, j * LANES : (j + 1) * LANES
-                ].astype(F32)
+                spot = pl.ds(pl.multiple_of(s * channels, channels), channels)
+                wide_in[j, spot, :] = landing[spot, j * LANES : (j + 1) * LANES].astype(F32)
             return carry
 
         lax.fori_loop(0, sources, body, 0)
@@ -446,80 +475,39 @@
     summed = (mine + z_recv[...].astype(F32)) * scale
     gfilter[...] = summed
 
-    conv_arrive()
-    bconv_arrive()
+    def results(which, landing, parts):
+        lane = pl.ds(pl.multiple_of(which * LANES, LANES), LANES)
+        for i in range(3):
+            spot = pl.ds(i * LANES, LANES)
+            rows = landing[lane, spot].astype(F32).T
+            for other, held in parts:
+                held[spot, lane] = (other[spot, lane].astype(F32) * rows).astype(BF16)
+
     gate_leave()
     back_leave()
+    conv_arrive()
+
+    def conv_results(which, carry):
+        results(which, conv_recv, [(query, out), (cotan, gquery)])
+        return carry
+
+    lax.fori_loop(0, 4, conv_results, 0)
     conv_leave()
+    for dz in far_first:
+        bconv_arrive(dz)
+        results(lax.rem(z + 4 - dz, 4), bconv_recv, [(value, gkey), (key, gvalue)])
     bconv_leave()
 
 
-def finish(
-    conv_hbm,
-    bconv_hbm,
-    term_hbm,
-    query_hbm,
-    key_hbm,
-    value_hbm,
-    cotan_hbm,
-    out_hbm,
-    gquery_hbm,
-    gkey_hbm,
-    gvalue_hbm,
-    gfilter_hbm,
-    conv,
-    bconv,
-    term,
-    query,
-    key,
-    value,
-    cotan,
-    out_buf,
-    load_sem,
-    store_sem,
-):
-    loads = []
-    for index, (src, dst) in enumerate(
-        [
-            (bconv_hbm, bconv),
-            (key_hbm, key),
-            (value_hbm, value),
-            (conv_hbm, conv),
-            (query_hbm, query),
-            (cotan_hbm, cotan),
-            (term_hbm, term),
-        ]
-    ):
-        load = pltpu.make_async_copy(src, dst, load_sem.at[index])
-        load.start()
-        loads.append(load)
-    stores = []
-
-    def results(landing, parts):
-        for c in range(query.shape[1] // LANES):
-            lane = slice(c * LANES, (c + 1) * LANES)
-            for i in range(3):
-                spot = slice(i * LANES, (i + 1) * LANES)
-                rows = landing[lane, spot].astype(F32).T
-                for which, other, dst in parts:
-                    out_buf[which, spot, lane] = (other[spot, lane].astype(F32) * rows).astype(BF16)
-            for which, other, dst in parts:
-                copy = pltpu.make_async_copy(
-                    out_buf.at[which, :, lane], dst.at[:, lane], store_sem.at[which, c]
-                )
-                copy.start()
-                stores.append(copy)
-
-    for load in loads[:3]:
-        load.wait()
-    results(bconv, [(2, value, gkey_hbm), (3, key, gvalue_hbm)])
-    for load in loads[3:]:
-        load.wait()
-    copy = pltpu.make_async_copy(term, gfilter_hbm, load_sem.at[0])
-    copy.start()
-    stores.append(copy)
-    results(conv, [(0, query, out_hbm), (1, cotan, gquery_hbm)])
-    for copy in stores:
+def store(*refs):
+    held, results, sems = refs[:5], refs[5:10], refs[10]
+    copies = [
+        pltpu.make_async_copy(src, dst, sems.at[index])
+        for index, (src, dst) in enumerate(zip(held, results))
+    ]
+    for copy in copies:
+        copy.start()
+    for copy in copies:
         copy.wait()
 
 
@@ -531,15 +519,14 @@
     rows = sources * 3
     scale = 1.0 / math.sqrt(lax.axis_size("rep") * tokens * sources)
     anywhere = pl.BlockSpec(memory_space=pl.ANY)
-    block = (sources, channels, tokens)
-    landing = jax.ShapeDtypeStruct(block, BF16)
+    inside = pl.BlockSpec(memory_space=pltpu.VMEM)
     vmem = pltpu.VMEM
     features = (query_feat[0], key_feat[0], value_feat[0], out_cotangent[0])
-    conv, bconv, term = pl.pallas_call(
+    held = pl.pallas_call(
         functools.partial(kernel, scale, sources, channels),
-        out_shape=(landing, landing, jax.ShapeDtypeStruct((channels, tokens), F32)),
+        out_shape=(*[vmem((tokens, width), BF16)] * 4, vmem((channels, tokens), F32)),
         in_specs=[pl.BlockSpec(memory_space=pltpu.HBM)] * 6,
-        out_specs=(anywhere, anywhere, pl.BlockSpec(memory_space=pltpu.VMEM)),
+        out_specs=(inside,) * 5,
         scratch_shapes=[
             *[vmem((tokens, width), BF16)] * 4,
             vmem(filter_taps.shape[::-1], F32),
@@ -551,8 +538,10 @@
             vmem((2, HALF, LANES), F32),
             vmem((width, tokens), BF16),
             vmem((width, tokens), BF16),
-            vmem(block, BF16),
-            vmem(block, BF16),
+            vmem((width, tokens), BF16),
+            vmem((width, tokens), BF16),
+            vmem((width, tokens), BF16),
+            vmem((width, tokens), BF16),
             vmem((width, tokens), BF16),
             vmem((width, tokens), BF16),
             vmem((3, sources * channels, LANES), F32),
@@ -568,8 +557,9 @@
             vmem((8, channels, tokens), F32),
             pltpu.SemaphoreType.DMA((6,)),
             pltpu.SemaphoreType.DMA((4,)),
-            pltpu.SemaphoreType.DMA((4, sources)),
-            pltpu.SemaphoreType.DMA((4, sources)),
+            pltpu.SemaphoreType.DMA((4,)),
+            pltpu.SemaphoreType.DMA((3,)),
+            pltpu.SemaphoreType.DMA((4,)),
             pltpu.SemaphoreType.DMA((5,)),
             pltpu.SemaphoreType.DMA((5,)),
         ],
@@ -579,21 +569,13 @@
     )(*features, filter_taps.T, jnp.asarray(tables))
     seq = jax.ShapeDtypeStruct((tokens, width), BF16)
     outs = pl.pallas_call(
-        finish,
+        store,
         out_shape=(seq, seq, seq, seq, jax.ShapeDtypeStruct((channels, tokens), F32)),
-        in_specs=[anywhere] * 7,
+        in_specs=[inside] * 5,
         out_specs=(anywhere,) * 5,
-        scratch_shapes=[
-            vmem((width, tokens), BF16),
-            vmem((width, tokens), BF16),
-            vmem((channels, tokens), F32),
-            *[vmem((tokens, width), BF16)] * 4,
-            vmem((4, tokens, width), BF16),
-            pltpu.SemaphoreType.DMA((7,)),
-            pltpu.SemaphoreType.DMA((4, width // LANES)),
-        ],
-        compiler_params=pltpu.CompilerParams(vmem_limit_bytes=60 * 2**20),
-    )(conv.reshape(width, tokens), bconv.reshape(width, tokens), term, *features)
+        scratch_shapes=[pltpu.SemaphoreType.DMA((5,))],
+        compiler_params=pltpu.CompilerParams(vmem_limit_bytes=4 * 2**20),
+    )(*held)
     return (*[out[None] for out in outs[:4]], outs[4].T)
 
 

time: 54.8 us -> 49.7 us (0.907)
  the two profiles are of different devices: /device:TPU:24 before, /device:TPU:1 now
where the time goes in v2:
time: 49.7 us; the launch traced here: 49.6 us
  Pallas kernels  49 us (99%)
  between operations  0.64 us (1%)
    pallas_call x1, Pallas kernels, on_device(): pl.pallas_call(functools.partial(kernel, scale, sources, channels), out_s...  47.8 us
    pallas_call x1, Pallas kernels, on_device(): pl.pallas_call(store, out_shape=(seq, seq, seq, seq, jax.ShapeDtypeStruct...  1.18 us

profile of v2, /device:TPU:1, one launch (start us, length us, event | category | flops | bytes accessed | tf_op | source)
XLA Modules:
  0.0 49.6 jit_solution(2536203233578064036)
XLA Ops:
  0.6 47.8 %shard_map.101 = (bf16[384,512]{1,0:T(8,128)(2,1)S(1)}, bf16[384,512]{1,0:T(8,128)(2,1)S(1)}, bf16[384,512]{1,0:T(8,128)(2,1)S(1)}, bf16[384,512]{1,0:T(8,128)(2,1)S(1)}, f32[32,384]{1,0:T(8,128)S(1)}) custom-call(bf16[384,512]{1,0:T(8,128)(2,1)} %bitcast.11, bf16[384,512]{1,0:T(8,128)(2,1)} %bitcast.12, bf16[384,512]{1,0:T(8,128)(2,1)} %bitcast.13, ...), custom_call_target="tpu_custom_call" | custom-call | tf_op jit(solution)/shard_map/pallas_call | solution.py:525
  48.4 1.2 %shard_map.102 = (bf16[384,512]{1,0:T(8,128)(2,1)}, bf16[384,512]{1,0:T(8,128)(2,1)}, bf16[384,512]{1,0:T(8,128)(2,1)}, bf16[384,512]{1,0:T(8,128)(2,1)}, f32[32,384]{1,0:T(8,128)}) custom-call(bf16[384,512]{1,0:T(8,128)(2,1)S(1)} %get-tuple-element.15.refs_0_, bf16[384,512]{1,0:T(8,128)(2,1)S(1)} %get-tuple-element.16.refs_1_, ...), custom_call_target="tpu_custom_call" | custom-call | tf_op jit(solution)/shard_map/pallas_call | solution.py:571

commit v3 on v2

--- a/solution.py
+++ b/solution.py
@@ -172,6 +172,7 @@
     last_sem,
     red_send,
     red_recv,
+    x_ready,
 ):
     me = lax.axis_index("ctx")
     rep = lax.axis_index("rep")
@@ -183,22 +184,32 @@
     tokens = 3 * LANES
     groups = channels // GROUP
 
-    barrier = pltpu.get_barrier_semaphore()
-
-    def greet(step, carry):
-        peer = lax.rem(me + step, sources)
-        pl.semaphore_signal(barrier, inc=1, device_id=(rep, peer), device_id_type=MESH)
-        return carry
-
     other_core = rep + 1 - 2 * core
     other_z = (1 - zl) * 8 + xc * 2 + core
 
-    def x_peer(step):
-        return zl * 8 + lax.rem(xc + step, 4) * 2 + core
-
-    lax.fori_loop(1, sources, greet, 0)
-    for peer in [other_core, other_z] + [x_peer(step) for step in range(1, 4)]:
+    def x_peer(where):
+        return zl * 8 + where * 2 + core
+
+    barrier = pltpu.get_barrier_semaphore()
+
+    def greet(peer, carry):
+        pl.semaphore_signal(barrier, inc=1, device_id=(rep, peer), device_id_type=MESH)
+        return carry
+
+    def greet_x(where, carry):
+        pl.semaphore_signal(barrier, inc=1, device_id=(x_peer(where), me), device_id_type=MESH)
+        return carry
+
+    lax.fori_loop(1, sources, lambda step, carry: greet(lax.rem(me + step, sources), carry), 0)
+    lax.fori_loop(xc + 1, 4, greet_x, 0)
+    for peer in (other_core, other_z):
         pl.semaphore_signal(barrier, inc=1, device_id=(peer, me), device_id_type=MESH)
+
+    def report_x(where, carry):
+        pl.semaphore_signal(
+            x_ready.at[xc], inc=1, device_id=(x_peer(where), me), device_id_type=MESH
+        )
+        return carry
 
     loads = []
     for index, (src, dst) in enumerate(
@@ -226,7 +237,7 @@
 
         lax.fori_loop(0, left.shape[1] // LANES, body, 0)
 
-    far_first = (2, 1, 3, 0)
+    far_first = (0, 1, 3, 2)
 
     def own(kind, held, landing):
         return pltpu.make_async_copy(
@@ -302,16 +313,13 @@
     loads[0].wait()
     loads[1].wait()
     products(key, value, gate_send)
-    with jax.named_scope("barrier"):
-        pl.semaphore_wait(barrier, sources - 1 + 5)
-    with jax.named_scope("gate_go"):
-        gate_go()
+    pl.semaphore_wait(barrier, sources + 1 + xc)
+    gate_go()
+    lax.fori_loop(0, xc, report_x, 0)
     loads[2].wait()
     loads[3].wait()
-    with jax.named_scope("back_products"):
-        products(cotan, query, back_send)
-    with jax.named_scope("back_go"):
-        back_go()
+    products(cotan, query, back_send)
+    back_go()
 
     loads[4].wait()
     loads[5].wait()
@@ -438,34 +446,46 @@
         return carry
 
     lax.fori_loop(0, 8, add_core, 0)
-    x_copies = []
-    for step in range(1, 4):
-        there = lax.rem(xc + step, 4)
-        copy = pltpu.make_async_remote_copy(
-            src_ref=x_send.at[pl.ds(there * 2, 2)],
-            dst_ref=x_recv.at[step - 1],
-            send_sem=red_send.at[step],
-            recv_sem=red_recv.at[step],
-            device_id=(x_peer(step), me),
+
+    def x_copy(where, sender, block):
+        return pltpu.make_async_remote_copy(
+            src_ref=x_send.at[pl.ds(block * 2, 2)],
+            dst_ref=x_recv.at[sender],
+            send_sem=red_send.at[1 + block],
+            recv_sem=red_recv.at[1 + sender],
+            device_id=(x_peer(where), me),
             device_id_type=MESH,
         )
-        copy.start()
-        x_copies.append(copy)
-    for copy in x_copies:
-        copy.wait()
+
+    def x_start(where, carry):
+        x_copy(where, xc, where).start()
+        return carry
+
+    def x_start_when_ready(where, carry):
+        pl.semaphore_wait(x_ready.at[where], 1)
+        return x_start(where, carry)
+
+    def x_wait(step, carry):
+        where = lax.rem(xc + step, 4)
+        x_copy(where, where, where).wait()
+        return carry
+
+    lax.fori_loop(0, xc, x_start, 0)
+    lax.fori_loop(xc + 1, 4, x_start_when_ready, 0)
+    lax.fori_loop(1, 4, x_wait, 0)
 
     def x_sum(which):
         added = total[xc * 2 + which]
-        for step in range(3):
-            added = added + x_recv[step, which].astype(F32)
+        for step in range(1, 4):
+            added = added + x_recv[lax.rem(xc + step, 4), which].astype(F32)
         return added
 
     z_send[...] = x_sum(1 - zl).astype(BF16)
     z_copy = pltpu.make_async_remote_copy(
         src_ref=z_send,
         dst_ref=z_recv,
-        send_sem=red_send.at[4],
-        recv_sem=red_recv.at[4],
+        send_sem=red_send.at[5],
+        recv_sem=red_recv.at[5],
         device_id=(other_z, me),
         device_id_type=MESH,
     )
@@ -551,7 +571,7 @@
             vmem((8, channels, tokens), BF16),
             vmem((8, channels, tokens), BF16),
             vmem((8, channels, tokens), BF16),
-            vmem((3, 2, channels, tokens), BF16),
+            vmem((4, 2, channels, tokens), BF16),
             vmem((channels, tokens), BF16),
             vmem((channels, tokens), BF16),
             vmem((8, channels, tokens), F32),
@@ -560,8 +580,9 @@
             pltpu.SemaphoreType.DMA((4,)),
             pltpu.SemaphoreType.DMA((3,)),
             pltpu.SemaphoreType.DMA((4,)),
-            pltpu.SemaphoreType.DMA((5,)),
-            pltpu.SemaphoreType.DMA((5,)),
+            pltpu.SemaphoreType.DMA((6,)),
+            pltpu.SemaphoreType.DMA((6,)),
+            pltpu.SemaphoreType.REGULAR((4,)),
         ],
         compiler_params=pltpu.CompilerParams(
             collective_id=0, has_side_effects=True, vmem_limit_bytes=60 * 2**20

time: 49.7 us -> 48.9 us (0.984)
  Pallas kernels: 49 us -> 48 us
    pallas_call x1, Pallas kernels: 47.8 us -> 46.8 us  [on_device(): pl.pallas_call(functools.partial(kernel, scale, sources, channels), out_s...]
where the time goes in v3:
time: 48.9 us; the launch traced here: 48.6 us
  Pallas kernels  48 us (98%)
  between operations  0.64 us (1%)
    pallas_call x1, Pallas kernels, on_device(): pl.pallas_call(functools.partial(kernel, scale, sources, channels), out_s...  46.8 us
    pallas_call x1, Pallas kernels, on_device(): pl.pallas_call(store, out_shape=(seq, seq, seq, seq, jax.ShapeDtypeStruct...  1.18 us

profile of v3, /device:TPU:1, one launch (start us, length us, event | category | flops | bytes accessed | tf_op | source)
XLA Modules:
  0.0 48.6 jit_solution(13909337217930260666)
XLA Ops:
  0.6 46.8 %shard_map.101 = (bf16[384,512]{1,0:T(8,128)(2,1)S(1)}, bf16[384,512]{1,0:T(8,128)(2,1)S(1)}, bf16[384,512]{1,0:T(8,128)(2,1)S(1)}, bf16[384,512]{1,0:T(8,128)(2,1)S(1)}, f32[32,384]{1,0:T(8,128)S(1)}) custom-call(bf16[384,512]{1,0:T(8,128)(2,1)} %bitcast.11, bf16[384,512]{1,0:T(8,128)(2,1)} %bitcast.12, bf16[384,512]{1,0:T(8,128)(2,1)} %bitcast.13, ...), custom_call_target="tpu_custom_call" | custom-call | tf_op jit(solution)/shard_map/pallas_call | solution.py:545
  47.5 1.2 %shard_map.102 = (bf16[384,512]{1,0:T(8,128)(2,1)}, bf16[384,512]{1,0:T(8,128)(2,1)}, bf16[384,512]{1,0:T(8,128)(2,1)}, bf16[384,512]{1,0:T(8,128)(2,1)}, f32[32,384]{1,0:T(8,128)}) custom-call(bf16[384,512]{1,0:T(8,128)(2,1)S(1)} %get-tuple-element.15.refs_0_, bf16[384,512]{1,0:T(8,128)(2,1)S(1)} %get-tuple-element.16.refs_1_, ...), custom_call_target="tpu_custom_call" | custom-call | tf_op jit(solution)/shard_map/pallas_call | solution.py:592

commit v4 on v3

--- a/solution.py
+++ b/solution.py
@@ -54,12 +54,14 @@
     back = np.block([[cos, sin], [-sin, cos]])
 
     first_high, first_low = split_table(first)
+    middle_high, middle_low = split_table(middle)
+    back_high, back_low = split_table(back)
     last_high, last_low = split_table(last)
     parts = (
         np.concatenate([first_high, first_low, first_high], axis=1),
         np.concatenate([last_high, last_low], axis=1),
-        middle,
-        back,
+        np.concatenate([middle_high, middle_low]),
+        np.concatenate([back_high, back_low]),
         np.concatenate([twist[0], twist[1]], axis=1),
     )
     width = 2 * LANES
@@ -70,6 +72,24 @@
 
 def dot(left, right):
     return jnp.dot(left, right, preferred_element_type=F32)
+
+
+def two_parts(wide):
+    high = wide.astype(BF16)
+    return high, (wide - high.astype(F32)).astype(BF16)
+
+
+def exact_dot(left, table):
+    high, low = two_parts(left)
+    return (
+        dot(high, table[: 2 * LANES, :])
+        + dot(low, table[: 2 * LANES, :])
+        + dot(high, table[2 * LANES :, :])
+    )
+
+
+def rounded_dot(left, table):
+    return dot(left.astype(BF16), table[: 2 * LANES, :])
 
 
 def take_rows(wide, group, sources, channels):
@@ -93,7 +113,7 @@
             ]
 
 
-def forward(stacked, first, twist, middle):
+def forward(stacked, first, twist, middle, multiply):
     cos, sin = twist[0], twist[1]
     waves = dot(first, stacked)
     rows = []
@@ -103,12 +123,12 @@
         rows.append(
             jnp.concatenate([real * cos + imag * sin, imag * cos - real * sin], axis=1)
         )
-    return dot(jnp.concatenate(rows, axis=0).astype(BF16), middle)
+    return multiply(jnp.concatenate(rows, axis=0), middle)
 
 
 def inverse(real, imag, back, twist, last):
     cos, sin = twist[0], twist[1]
-    turned = dot(jnp.concatenate([real, imag], axis=1).astype(BF16), back)
+    turned = rounded_dot(jnp.concatenate([real, imag], axis=1), back)
     columns = []
     for c in range(GROUP):
         zr = turned[c * HALF : (c + 1) * HALF, :LANES]
@@ -181,7 +201,6 @@
     zl = rep // 8
     xc = rep // 2 % 4
     core = rep % 2
-    tokens = 3 * LANES
     groups = channels // GROUP
 
     other_core = rep + 1 - 2 * core
@@ -237,7 +256,7 @@
 
         lax.fori_loop(0, left.shape[1] // LANES, body, 0)
 
-    far_first = (0, 1, 3, 2)
+    row_order = (0, 1, 3, 2)
 
     def own(kind, held, landing):
         return pltpu.make_async_copy(
@@ -259,7 +278,7 @@
     def exchange(kind, held, landing):
         def go():
             own(kind, held, landing).start()
-            for dz in far_first:
+            for dz in row_order:
 
                 def start(step, carry):
                     peer = lax.rem(z + dz, 4) * rows_of + lax.rem(y + step, rows_of)
@@ -293,7 +312,7 @@
 
     def bconv_go():
         own(3, bconv_send, bconv_recv).start()
-        for dz in far_first:
+        for dz in row_order:
 
             def start(step, carry):
                 peer = lax.rem(z + dz, 4) * rows_of + lax.rem(y + step, rows_of)
@@ -340,10 +359,9 @@
 
     def filter_group(g, carry):
         rows = take_rows(wide_in, g, sources, channels)
-        high = rows.astype(BF16)
-        low = (rows - high.astype(F32)).astype(BF16)
+        high, low = two_parts(rows)
         filt_spec[g] = forward(
-            jnp.concatenate([high, high, low], axis=0), first[...], twist, middle[...]
+            jnp.concatenate([high, high, low], axis=0), first[...], twist, middle, exact_dot
         )
         return carry
 
@@ -369,7 +387,7 @@
 
     def spectrum(g):
         rows = take_rows(wide_in, g, sources, channels).astype(BF16)
-        return forward(jnp.concatenate([rows, rows], axis=0), first[:, : 2 * sources * 3], twist, middle[...])
+        return forward(jnp.concatenate([rows, rows], axis=0), first[:, : 2 * sources * 3], twist, middle, rounded_dot)
 
     gate_arrive()
     widen(gate_recv)
@@ -379,7 +397,7 @@
         gate_spec[g] = spec
         gr, gi = spec[:, :LANES], spec[:, LANES:]
         hr, hi = filt_spec[g, :, :LANES], filt_spec[g, :, LANES:]
-        rows = inverse(gr * hr - gi * hi, gr * hi + gi * hr, back[...], twist, last[...])
+        rows = inverse(gr * hr - gi * hi, gr * hi + gi * hr, back, twist, last[...])
         put_rows(wide_out, g, sources, channels, rows)
         return carry
 
@@ -394,7 +412,7 @@
         spec = spectrum(g)
         br, bi = spec[:, :LANES], spec[:, LANES:]
         hr, hi = filt_spec[g, :, :LANES], filt_spec[g, :, LANES:]
-        rows = inverse(br * hr + bi * hi, bi * hr - br * hi, back[...], twist, last[...])
+        rows = inverse(br * hr + bi * hi, bi * hr - br * hi, back, twist, last[...])
         put_rows(wide_out, g, sources, channels, rows)
         gr, gi = gate_spec[g, :, :LANES], gate_spec[g, :, LANES:]
         gate_spec[g] = jnp.concatenate([br * gr + bi * gi, bi * gr - br * gi], axis=1)
@@ -406,7 +424,7 @@
 
     def term_group(g, carry):
         rows = inverse(
-            gate_spec[g, :, :LANES], gate_spec[g, :, LANES:], back[...], twist, last[...]
+            gate_spec[g, :, :LANES], gate_spec[g, :, LANES:], back, twist, last[...]
         )
         put_rows(wide_out, g, sources, channels, rows)
         return carry
@@ -513,7 +531,7 @@
 
     lax.fori_loop(0, 4, conv_results, 0)
     conv_leave()
-    for dz in far_first:
+    for dz in row_order:
         bconv_arrive(dz)
         results(lax.rem(z + 4 - dz, 4), bconv_recv, [(value, gkey), (key, gvalue)])
     bconv_leave()
@@ -553,8 +571,8 @@
             vmem(tables.shape, F32),
             vmem((2 * HALF, 3 * rows), BF16),
             vmem((rows, 4 * HALF), BF16),
-            vmem((2 * LANES, 2 * LANES), BF16),
-            vmem((2 * LANES, 2 * LANES), BF16),
+            vmem((4 * LANES, 2 * LANES), BF16),
+            vmem((4 * LANES, 2 * LANES), BF16),
             vmem((2, HALF, LANES), F32),
             vmem((width, tokens), BF16),
             vmem((width, tokens), BF16),

time: 48.9 us -> 48.9 us (level)
  no operation moved by 1% of the time
where the time goes in v4:
time: 48.9 us; the launch traced here: 48.6 us
  Pallas kernels  48 us (98%)
  between operations  0.64 us (1%)
    pallas_call x1, Pallas kernels, on_device(): pl.pallas_call(functools.partial(kernel, scale, sources, channels), out_s...  46.8 us
    pallas_call x1, Pallas kernels, on_device(): pl.pallas_call(store, out_shape=(seq, seq, seq, seq, jax.ShapeDtypeStruct...  1.18 us

profile of v4, /device:TPU:1, one launch (start us, length us, event | category | flops | bytes accessed | tf_op | source)
XLA Modules:
  0.0 48.6 jit_solution(12308053668943158024)
XLA Ops:
  0.6 46.8 %shard_map.101 = (bf16[384,512]{1,0:T(8,128)(2,1)S(1)}, bf16[384,512]{1,0:T(8,128)(2,1)S(1)}, bf16[384,512]{1,0:T(8,128)(2,1)S(1)}, bf16[384,512]{1,0:T(8,128)(2,1)S(1)}, f32[32,384]{1,0:T(8,128)S(1)}) custom-call(bf16[384,512]{1,0:T(8,128)(2,1)} %bitcast.11, bf16[384,512]{1,0:T(8,128)(2,1)} %bitcast.12, bf16[384,512]{1,0:T(8,128)(2,1)} %bitcast.13, ...), custom_call_target="tpu_custom_call" | custom-call | tf_op jit(solution)/shard_map/pallas_call | solution.py:563
  47.5 1.2 %shard_map.102 = (bf16[384,512]{1,0:T(8,128)(2,1)}, bf16[384,512]{1,0:T(8,128)(2,1)}, bf16[384,512]{1,0:T(8,128)(2,1)}, bf16[384,512]{1,0:T(8,128)(2,1)}, f32[32,384]{1,0:T(8,128)}) custom-call(bf16[384,512]{1,0:T(8,128)(2,1)S(1)} %get-tuple-element.15.refs_0_, bf16[384,512]{1,0:T(8,128)(2,1)S(1)} %get-tuple-element.16.refs_1_, ...), custom_call_target="tpu_custom_call" | custom-call | tf_op jit(solution)/shard_map/pallas_call | solution.py:610

commit v5 on v4

--- a/solution.py
+++ b/solution.py
@@ -278,14 +278,15 @@
     def exchange(kind, held, landing):
         def go():
             own(kind, held, landing).start()
-            for dz in row_order:
-
-                def start(step, carry):
+            for turn in row_order:
+                dz = lax.select(core == 0, turn, (4 - turn) % 4)
+
+                def start(step, carry, dz=dz):
                     peer = lax.rem(z + dz, 4) * rows_of + lax.rem(y + step, rows_of)
                     copies(kind, held, landing, 1, peer, peer, me).start()
                     return carry
 
-                lax.fori_loop(0 if dz else 1, rows_of, start, 0)
+                lax.fori_loop(0 if turn else 1, rows_of, start, 0)
 
         def whole():
             return copies(kind, held, landing, sources - 1, lax.rem(me + 1, sources), 0, 0)
@@ -312,14 +313,15 @@
 
     def bconv_go():
         own(3, bconv_send, bconv_recv).start()
-        for dz in row_order:
-
-            def start(step, carry):
+        for turn in row_order:
+            dz = lax.select(core == 0, turn, (4 - turn) % 4)
+
+            def start(step, carry, dz=dz):
                 peer = lax.rem(z + dz, 4) * rows_of + lax.rem(y + step, rows_of)
                 last_copy(1, dz, peer, peer, me).start()
                 return carry
 
-            lax.fori_loop(0 if dz else 1, rows_of, start, 0)
+            lax.fori_loop(0 if turn else 1, rows_of, start, 0)
 
     def bconv_arrive(dz):
         if dz == 0:
@@ -332,13 +334,13 @@
     loads[0].wait()
     loads[1].wait()
     products(key, value, gate_send)
-    pl.semaphore_wait(barrier, sources + 1 + xc)
-    gate_go()
-    lax.fori_loop(0, xc, report_x, 0)
     loads[2].wait()
     loads[3].wait()
     products(cotan, query, back_send)
+    pl.semaphore_wait(barrier, sources + 1 + xc)
+    gate_go()
     back_go()
+    lax.fori_loop(0, xc, report_x, 0)
 
     loads[4].wait()
     loads[5].wait()

time: 48.9 us -> 49.8 us (1.018)
  Pallas kernels: 48 us -> 49 us
    pallas_call x1, Pallas kernels: 46.8 us -> 47.9 us  [on_device(): pl.pallas_call(functools.partial(kernel, scale, sources, channels), out_s...]
where the time goes in v5:
time: 49.8 us; the launch traced here: 49.7 us
  Pallas kernels  49 us (98%)
  between operations  0.64 us (1%)
    pallas_call x1, Pallas kernels, on_device(): pl.pallas_call(functools.partial(kernel, scale, sources, channels), out_s...  47.9 us
    pallas_call x1, Pallas kernels, on_device(): pl.pallas_call(store, out_shape=(seq, seq, seq, seq, jax.ShapeDtypeStruct...  1.18 us

profile of v5, /device:TPU:1, one launch (start us, length us, event | category | flops | bytes accessed | tf_op | source)
XLA Modules:
  0.0 49.7 jit_solution(3535925488237330190)
XLA Ops:
  0.6 47.9 %shard_map.101 = (bf16[384,512]{1,0:T(8,128)(2,1)S(1)}, bf16[384,512]{1,0:T(8,128)(2,1)S(1)}, bf16[384,512]{1,0:T(8,128)(2,1)S(1)}, bf16[384,512]{1,0:T(8,128)(2,1)S(1)}, f32[32,384]{1,0:T(8,128)S(1)}) custom-call(bf16[384,512]{1,0:T(8,128)(2,1)} %bitcast.11, bf16[384,512]{1,0:T(8,128)(2,1)} %bitcast.12, bf16[384,512]{1,0:T(8,128)(2,1)} %bitcast.13, ...), custom_call_target="tpu_custom_call" | custom-call | tf_op jit(solution)/shard_map/pallas_call | solution.py:565
  48.5 1.2 %shard_map.102 = (bf16[384,512]{1,0:T(8,128)(2,1)}, bf16[384,512]{1,0:T(8,128)(2,1)}, bf16[384,512]{1,0:T(8,128)(2,1)}, bf16[384,512]{1,0:T(8,128)(2,1)}, f32[32,384]{1,0:T(8,128)}) custom-call(bf16[384,512]{1,0:T(8,128)(2,1)S(1)} %get-tuple-element.15.refs_0_, bf16[384,512]{1,0:T(8,128)(2,1)S(1)} %get-tuple-element.16.refs_1_, ...), custom_call_target="tpu_custom_call" | custom-call | tf_op jit(solution)/shard_map/pallas_call | solution.py:612
